TPU v7x, 128 devices: a whole 4x4x4 slice. The times are simulated.
128 devices in a mesh: tm: 16 (over x, z), batch: 8 (over y, core).
Axes of the slice: x: 4, y: 4, z: 4, core: 2. Of those that a mesh axis runs over, the one named last changes fastest.
Arguments:
- state: float32 [16, 8, 256, 1152], P('tm', 'batch'), may hold values from -6 to 6
- noise_draws: bfloat16 [2, 16, 8, 256, 1152], P(None, 'tm', 'batch'), may hold values from -6 to 6
- class_vec: float32 [8, 1152], P('batch'), may hold values from -6 to 6
- window_start: int32 [8], P('batch'), may hold values from 0 to 977
- advance: int32 [8], P('batch'), may hold values from 1 to 7
- step_dt: float32 [1000], replicated, may hold values from 0.05 to 0.2
- step_sigma: float32 [1000], replicated, may hold values from 0.05 to 0.2
- w_ada: bfloat16 [1152, 3456], replicated, may hold values from -0.1875 to 0.1875
- w_up: bfloat16 [4608, 1152], P(('tm', 'batch')), may hold values from -0.1875 to 0.1875
- w_down: bfloat16 [4608, 1152], P(('tm', 'batch')), may hold values from -0.09375 to 0.09375
Outputs:
- window_out: float32 [16, 8, 256, 1152], P('tm', 'batch')
All inputs are finite; a program needn't handle non-finite values.
Results may differ from a plain program's by a relative error of at most 0.0037.
Values may be sent and summed in bfloat16 or wider, within the bound.
No kernel may reach another device: no remote copies, remote signals or barrier semaphores. Data moves between devices by JAX's collectives and lax.ppermute only.
A program may use at most 128 MiB of HBM per device.

v0:
```python
import math
import jax
import jax.numpy as jnp
from jax import lax
from jax.sharding import PartitionSpec as P

SLIDE_BITS = 3
EPSILON = 1e-06


def spread_2(shard, axis, root):
    mine = lax.axis_index(axis) == root
    return lax.psum(jnp.where(mine, shard, jnp.zeros_like(shard)), axis)


def carried_in(part, axis, combine, identity):
    place = lax.axis_index(axis)
    gathered = lax.all_gather(part, axis)
    state = jnp.zeros_like(part) + jnp.asarray(identity, part.dtype)

    def one(turn, state):
        return combine(state, lax.dynamic_index_in_dim(gathered, turn, 0, False))

    return lax.fori_loop(0, place, one, state)


def from_behind(shard, axis, by):
    peers = lax.axis_size(axis)
    pairs = [(i, i + by) for i in range(peers) if 0 <= i + by < peers]
    return lax.ppermute(shard, axis, pairs)


def time_embed(steps_now, half_width):
    frequency = jnp.exp(-math.log(10000.0) * jnp.arange(half_width, dtype=jnp.float32) / half_width)
    angles = steps_now.astype(jnp.float32)[:, None] * frequency[None, :]
    return jnp.concatenate([jnp.cos(angles), jnp.sin(angles)], axis=1)


def dense_pair(hidden_rows, up_rows, down_rows):
    before = lax.dot_general(
        hidden_rows, up_rows, (((1,), (1,)), ((), ())), preferred_element_type=jnp.float32
    )
    activated = jax.nn.gelu(before, approximate=True).astype(jnp.bfloat16)
    return jnp.dot(activated, down_rows, preferred_element_type=jnp.float32)


def combine_sum(earlier, later):
    return earlier + later


def increment(current, noise_now, steps_now, class_vec, step_dt, step_sigma, w_ada, mlp_apply):
    images, tokens, channels = current.shape
    step_table = lax.iota(jnp.int32, step_dt.shape[0])
    onehot = (steps_now[:, None] == step_table[None, :]).astype(jnp.float32)
    step_size = jnp.sum(onehot * step_dt[None, :], axis=1)
    spread = jnp.sum(onehot * step_sigma[None, :], axis=1)
    condition = jax.nn.silu(time_embed(steps_now, channels // 2) + class_vec).astype(jnp.bfloat16)
    modulation = jnp.dot(condition, w_ada, preferred_element_type=jnp.float32)
    shift_by = modulation[:, :channels]
    scale_by = modulation[:, channels : 2 * channels]
    gate_by = modulation[:, 2 * channels :]
    mean_val = jnp.mean(current, axis=2, keepdims=True)
    centred = current - mean_val
    var_val = jnp.mean(centred * centred, axis=2, keepdims=True)
    normed = centred * lax.rsqrt(var_val + EPSILON)
    hidden_in = (normed * (1.0 + scale_by[:, None, :]) + shift_by[:, None, :]).astype(jnp.bfloat16)
    mlp_out = mlp_apply(hidden_in.reshape(images * tokens, channels)).reshape(
        images, tokens, channels
    )
    drift = gate_by[:, None, :] * mlp_out - current
    return step_size[:, None, None] * drift + spread[:, None, None] * noise_now.astype(jnp.float32)


def per_device(
    state, noise_draws, class_vec, window_start, advance, step_dt, step_sigma, w_ada, w_up, w_down
):
    window_size = lax.axis_size("tm")
    position = lax.axis_index("tm")
    up_whole, down_whole = (
        lax.all_gather(w_up, ("tm", "batch"), axis=0, tiled=True),
        lax.all_gather(w_down, ("tm", "batch"), axis=0, tiled=True),
    )

    def mlp_apply(hidden_rows):
        return dense_pair(hidden_rows, up_whole, down_whole)

    def sweep(current, noise_now, starts):
        steps_now = starts + position
        step_inc = increment(
            current, noise_now, steps_now, class_vec, step_dt, step_sigma, w_ada, mlp_apply
        )
        base_rows = spread_2(current, "tm", 0)
        prefix = carried_in(step_inc, "tm", combine_sum, jnp.zeros_like(step_inc))
        updated = base_rows + prefix
        return (updated, step_inc)

    updated, step_inc = sweep(state[0], noise_draws[0, 0], window_start)
    end_rows = updated + step_inc
    tail_rows = jnp.where(position == window_size - 1, end_rows, jnp.zeros_like(end_rows))
    moved = updated
    for section_bit in range(SLIDE_BITS):
        distance = 1 << section_bit
        arrived, arrived_tail = from_behind((moved, tail_rows), "tm", -distance)
        taken = advance >> section_bit & 1 == 1
        outside = position + distance >= window_size
        incoming = jnp.where(outside, tail_rows, arrived)
        moved = jnp.where(taken[:, None, None], incoming, moved)
        tail_rows = jnp.where(position >= window_size - distance, tail_rows, arrived_tail)
    final_rows, leftover = sweep(moved, noise_draws[1, 0], window_start + advance)
    return final_rows[None]


def solution(mesh):
    in_specs = (
        P("tm", "batch", None, None),
        P(None, "tm", "batch", None, None),
        P("batch", None),
        P("batch"),
        P("batch"),
        P(),
        P(),
        P(),
        P(("tm", "batch"), None),
        P(("tm", "batch"), None),
    )
    out_specs = P("tm", "batch", None, None)
    return jax.shard_map(
        per_device, mesh=mesh, in_specs=in_specs, out_specs=out_specs, check_vma=False
    )
```

profile of v0, /device:TPU:0, one launch (start us, length us, event | category | flops | bytes accessed | tf_op | source)
XLA Modules:
  0.0 791.6 jit_solution(7158159004411722302)
XLA Ops:
  6.5 0.7 all-gather.15.cloned.1.call-update
  7.3 0.0 all-gather.13.cloned.1.call-start
  7.3 0.7 all-gather.13.cloned.1.call-update
  8.0 0.0 all-gather.9.cloned.1.call-start
  9.4 1.4 reduce_sum.73
  10.8 0.1 fusion.87
  10.9 0.7 select_reduce_fusion
  11.6 4.5 fusion.73
  16.2 1.2 fusion.39
  17.4 68.0 %all-gather.15.cloned.1.call-done = bf16[128,36,1152]{2,1,0:T(8,128)(2,1)} async-done(((bf16[1,36,1152]{2,1,0:T(8,128)(2,1)}), bf16[128,36,1152]{2,1,0:T(8,128)(2,1)}) %all-gather.15.cloned.1.call-update) | async-done | bytes 10616848 | tf_op jit(solution)/shard_map/all_gather | solution.py:81
  85.3 16.3 %reshape.304 = bf16[4608,1152]{1,0:T(8,128)(2,1)} reshape(bf16[128,36,1152]{2,1,0:T(8,128)(2,1)} %all-gather.15.cloned.1.call-done) | data formatting | bytes 21233664
  101.6 58.2 %all-gather.13.cloned.1.call-done = bf16[128,36,1152]{2,1,0:T(8,128)(2,1)} async-done(((bf16[1,36,1152]{2,1,0:T(8,128)(2,1)}), bf16[128,36,1152]{2,1,0:T(8,128)(2,1)}) %all-gather.13.cloned.1.call-update) | async-done | bytes 10616848 | tf_op jit(solution)/shard_map/all_gather | solution.py:80
  159.9 16.3 %reshape.302 = bf16[4608,1152]{1,0:T(8,128)(2,1)} reshape(bf16[128,36,1152]{2,1,0:T(8,128)(2,1)} %all-gather.13.cloned.1.call-done) | data formatting | bytes 21233664
  176.2 15.8 %fusion.18 = f32[256,1152]{1,0:T(8,128)} fusion(bf16[4608,1152]{1,0:T(8,128)(2,1)} %reshape.304, f32[1,1,256,1152]{3,2,1,0:T(8,128)S(1)} %copy-done.1, bf16[4608,1152]{1,0:T(8,128)(2,1)} %reshape.302, bf16[2,1,1,256,1152]{4,3,2,1,0:T(8,128)(2,1)S(1)} %copy-done.10, f32[]{:T(128)} %get-tuple-element.86, f32[1152]{0:T(1024)S(1)} %get-tuple-element.82, ...), kind=kOutput, calls=%fused_computation.24 | convolution fusion | flops 5449678848 | bytes 25389064 | tf_op jit(solution)/shard_map/dot_general | solution.py:44
  192.0 0.0 all-reduce.3.cloned.1.call-start
  192.1 0.5 all-reduce.3.cloned.1.call-update
  192.6 120.7 %all-gather.9.cloned.1.call-done = f32[4096,1152]{1,0:T(8,128)} async-done(((f32[256,1152]{1,0:T(8,128)}), f32[4096,1152]{1,0:T(8,128)}) %all-gather.9.cloned.1.call-update) | async-done | bytes 18874384 | tf_op jit(solution)/shard_map/all_gather | solution.py:18
  313.3 0.1 broadcast.231.clone
  313.4 89.8 %all-reduce.3.cloned.1.call-done = f32[1,256,1152]{2,1,0:T(8,128)} async-done(((f32[1,256,1152]{2,1,0:T(8,128)}), f32[1,256,1152]{2,1,0:T(8,128)}) %all-reduce.3.cloned.1.call-update) | async-done | bytes 1179664 | tf_op jit(solution)/shard_map/psum | solution.py:13
  403.2 1.5 add.160
  404.7 1.3 collective-permute-start.2
  406.0 26.8 %collective-permute-done.2 = f32[1,256,1152]{2,1,0:T(8,128)S(1)} collective-permute-done((f32[1,256,1152]{2,1,0:T(8,128)S(1)}, f32[1,256,1152]{2,1,0:T(8,128)S(1)}, u32[]{:S(2)}, u32[]{:S(2)}) %collective-permute-start.2) | collective-permute-done | bytes 1179680 | tf_op jit(solution)/shard_map/ppermute | solution.py:30
  432.8 1.0 copy-done.2
  433.9 2.5 select_select_fusion.2
  436.3 1.3 collective-permute-start.3
  437.6 1.3 collective-permute-start
  438.9 26.1 %collective-permute-done.3 = f32[1,256,1152]{2,1,0:T(8,128)S(1)} collective-permute-done((f32[1,256,1152]{2,1,0:T(8,128)S(1)}, f32[1,256,1152]{2,1,0:T(8,128)S(1)}, u32[]{:S(2)}, u32[]{:S(2)}) %collective-permute-start.3) | collective-permute-done | bytes 1179680 | tf_op jit(solution)/shard_map/ppermute | solution.py:30
  465.0 25.3 %collective-permute-done = f32[1,256,1152]{2,1,0:T(8,128)S(1)} collective-permute-done((f32[1,256,1152]{2,1,0:T(8,128)}, f32[1,256,1152]{2,1,0:T(8,128)S(1)}, u32[]{:S(2)}, u32[]{:S(2)}) %collective-permute-start) | collective-permute-done | bytes 1179680 | tf_op jit(solution)/shard_map/ppermute | solution.py:30
  490.3 1.0 copy-done.5
  491.4 1.9 select_select_fusion.1
  493.2 1.3 collective-permute-start.4
  494.5 1.5 collective-permute-start.1
  496.0 0.1 fusion.85
  496.1 4.4 fusion.71
  500.5 0.6 slice_reduce_fusion.1
  501.2 22.9 %collective-permute-done.4 = f32[1,256,1152]{2,1,0:T(8,128)S(1)} collective-permute-done((f32[1,256,1152]{2,1,0:T(8,128)S(1)}, f32[1,256,1152]{2,1,0:T(8,128)S(1)}, u32[]{:S(2)}, u32[]{:S(2)}) %collective-permute-start.4) | collective-permute-done | bytes 1179680 | tf_op jit(solution)/shard_map/ppermute | solution.py:30
  524.1 0.7 collective-permute-done.1
  524.8 0.3 copy-done.3
  525.1 1.9 fusion.101
  527.0 1.2 multiply_reduce_fusion
  528.2 0.4 copy-done.11
  528.6 15.9 %fusion.22 = f32[1,256,1152]{2,1,0:T(8,128)} fusion(f32[1,256,1152]{2,1,0:T(8,128)S(1)} %get-tuple-element.104, bf16[4608,1152]{1,0:T(8,128)(2,1)} %reshape.304, bf16[4608,1152]{1,0:T(8,128)(2,1)} %reshape.302, bf16[2,1,1,256,1152]{4,3,2,1,0:T(8,128)(2,1)S(1)} %copy-done.11, f32[]{:T(128)} %get-tuple-element.85, f32[1152]{0:T(1024)S(1)} %copy-done.7, ...), kind=kOutput, calls=%fused_computation.28 | convolution fusion | flops 5449678848 | bytes 25389064 | tf_op jit(solution)/shard_map/dot_general | solution.py:44
  544.5 0.0 all-reduce.5.cloned.1.call-start
  544.6 0.5 all-reduce.5.cloned.1.call-update
  545.1 147.3 %all-gather.11.cloned.1.call-done = f32[16,256,1152]{2,1,0:T(8,128)} async-done(((f32[1,256,1152]{2,1,0:T(8,128)}), f32[16,256,1152]{2,1,0:T(8,128)}) %all-gather.11.cloned.1.call-update) | async-done | bytes 18874384 | tf_op jit(solution)/shard_map/all_gather | solution.py:18
  692.4 0.1 broadcast.231
  692.5 89.8 %all-reduce.5.cloned.1.call-done = f32[1,256,1152]{2,1,0:T(8,128)} async-done(((f32[1,256,1152]{2,1,0:T(8,128)}), f32[1,256,1152]{2,1,0:T(8,128)}) %all-reduce.5.cloned.1.call-update) | async-done | bytes 1179664 | tf_op jit(solution)/shard_map/psum | solution.py:13
  782.3 2.4 add_bitcast_fusion
  (31 shorter events, 0.2 us)
Async XLA Ops:
  6.5 4.3 copy-start.8
  6.5 4.3 copy-start.9
  6.5 5.0 copy-start.6
  6.5 78.8 %all-gather.15.cloned.1.call-start = ((), (), s32[]{:S(2)}) async-start(), calls=%async_computation.5 | async-start | bytes 11888640 | tf_op jit(solution)/shard_map/all_gather | solution.py:81
  7.3 152.6 %all-gather.13.cloned.1.call-start = ((), (), s32[]{:S(2)}) async-start(), calls=%async_computation.4 | async-start | bytes 11888640 | tf_op jit(solution)/shard_map/all_gather | solution.py:80
  8.0 305.3 %all-gather.9.cloned.1.call-start = ((), (), s32[]{:S(2)}) async-start(), calls=%async_computation.2 | async-start | bytes 20054016 | tf_op jit(solution)/shard_map/all_gather | solution.py:18
  11.6 4.6 copy-start.1
  101.6 74.6 %copy-start.10 = (bf16[2,1,1,256,1152]{4,3,2,1,0:T(8,128)(2,1)S(1)}, bf16[2,1,1,256,1152]{4,3,2,1,0:T(8,128)(2,1)}, u32[]{:S(2)}) copy-start(bf16[2,1,1,256,1152]{4,3,2,1,0:T(8,128)(2,1)} %param.15) | copy-start | bytes 3538948
  192.0 211.2 %all-reduce.3.cloned.1.call-start = ((), (), s32[]{:S(2)}) async-start(), calls=%async_computation | async-start | bytes 2359296 | tf_op jit(solution)/shard_map/psum | solution.py:13
  192.6 499.8 %all-gather.11.cloned.1.call-start = ((), (), s32[]{:S(2)}) async-start(), calls=%async_computation.3 | async-start | bytes 20054016 | tf_op jit(solution)/shard_map/all_gather | solution.py:18
  403.2 30.6 %copy-start = (f32[256,1152]{1,0:T(8,128)S(1)}, f32[256,1152]{1,0:T(8,128)}, u32[]{:S(2)}) copy-start(f32[256,1152]{1,0:T(8,128)} %fusion.18) | copy-start | bytes 3538948
  404.7 28.1 %collective-permute-start.2 = (f32[1,256,1152]{2,1,0:T(8,128)S(1)}, f32[1,256,1152]{2,1,0:T(8,128)S(1)}, u32[]{:S(2)}, u32[]{:S(2)}) collective-permute-start(f32[1,256,1152]{2,1,0:T(8,128)S(1)} %add.160), channel_id=1, source_target_pairs={{8,0},{16,8},{24,16},{32,24},{40,32},{48,40},{56,48},{64,56},{72,6... | collective-permute-start | bytes 3538952 | tf_op jit(solution)/shard_map/ppermute | solution.py:30
  432.8 1.0 copy-start.2
  436.3 28.7 %collective-permute-start.3 = (f32[1,256,1152]{2,1,0:T(8,128)S(1)}, f32[1,256,1152]{2,1,0:T(8,128)S(1)}, u32[]{:S(2)}, u32[]{:S(2)}) collective-permute-start(f32[1,256,1152]{2,1,0:T(8,128)S(1)} %get-tuple-element.107), channel_id=1, source_target_pairs={{16,0},{24,8},{32,16},{40,24},{48,32},{56,40},{64,48},{72,56},{80,... | collective-permute-start | bytes 3538952 | tf_op jit(solution)/shard_map/ppermute | solution.py:30
  437.6 52.7 %collective-permute-start = (f32[1,256,1152]{2,1,0:T(8,128)}, f32[1,256,1152]{2,1,0:T(8,128)S(1)}, u32[]{:S(2)}, u32[]{:S(2)}) collective-permute-start(f32[1,256,1152]{2,1,0:T(8,128)} %get-tuple-element.108), channel_id=1, source_target_pairs={{8,0},{16,8},{24,16},{32,24},{40,32},{48,40},{56,48},{64,56},{72,6... | collective-permute-start | bytes 3538952 | tf_op jit(solution)/shard_map/ppermute | solution.py:30
  465.0 25.3 %copy-start.4 = (f32[1,256,1152]{2,1,0:T(8,128)}, f32[1,256,1152]{2,1,0:T(8,128)S(1)}, u32[]{:S(2)}) copy-start(f32[1,256,1152]{2,1,0:T(8,128)S(1)} %collective-permute-done.3) | copy-start | bytes 3538948
  490.3 1.1 copy-start.5
  493.2 30.8 %collective-permute-start.4 = (f32[1,256,1152]{2,1,0:T(8,128)S(1)}, f32[1,256,1152]{2,1,0:T(8,128)S(1)}, u32[]{:S(2)}, u32[]{:S(2)}) collective-permute-start(f32[1,256,1152]{2,1,0:T(8,128)S(1)} %get-tuple-element.105), channel_id=1, source_target_pairs={{32,0},{40,8},{48,16},{56,24},{64,32},{72,40},{80,48},{88,56},{96,... | collective-permute-start | bytes 3538952 | tf_op jit(solution)/shard_map/ppermute | solution.py:30
  494.5 30.3 %collective-permute-start.1 = (f32[1,256,1152]{2,1,0:T(8,128)S(1)}, f32[1,256,1152]{2,1,0:T(8,128)}, u32[]{:S(2)}, u32[]{:S(2)}) collective-permute-start(f32[1,256,1152]{2,1,0:T(8,128)S(1)} %get-tuple-element.106), channel_id=1, source_target_pairs={{16,0},{24,8},{32,16},{40,24},{48,32},{56,40},{64,48},{72,56},{80,... | collective-permute-start | bytes 3538952 | tf_op jit(solution)/shard_map/ppermute | solution.py:30
  524.1 1.0 copy-start.3
  527.0 1.2 copy-start.7
  527.0 1.6 copy-start.11
  544.5 237.8 %all-reduce.5.cloned.1.call-start = ((), (), s32[]{:S(2)}) async-start(), calls=%async_computation.1 | async-start | bytes 2359296 | tf_op jit(solution)/shard_map/psum | solution.py:13
Sparse Core Ops, SparseCore 0:
  10.3 74.9 all-gather.14
  88.3 71.5 all-gather.12
  192.1 121.1 all-gather.8
  316.5 86.6 all-reduce.2
  544.6 147.7 all-gather.10
  695.6 86.6 all-reduce.4
where the time goes:
time: 794 us; the launch traced here: 792 us
  waiting for transfers between devices  678 us (85%)
  matrix products  40.6 us (5%)
  local copies, waits for them, and re-layouts  35.5 us (4%)
  other arithmetic  15.6 us (2%)
  between operations  15 us (2%)
    all_gather x2, waiting for transfers between devices, carried_in(): gathered = lax.all_gather(part, axis)  268 us
    psum x2, waiting for transfers between devices, spread_2(): return lax.psum(jnp.where(mine, shard, jnp.zeros_like(shard)), axis)  180 us
    ppermute x5, waiting for transfers between devices, from_behind(): return lax.ppermute(shard, axis, pairs)  102 us
    all_gather x1, waiting for transfers between devices, per_device(): lax.all_gather(w_down, ('tm', 'batch'), axis=0, tiled=True)  68 us
    all_gather x1, waiting for transfers between devices, per_device(): lax.all_gather(w_up, ('tm', 'batch'), axis=0, tiled=True)  58.2 us
    unnamed x26, local copies, waits for them, and re-layouts  35.3 us
    dot_general x2, matrix products, dense_pair(): return jnp.dot(activated, down_rows, preferred_element_type=jnp.float32)  31.7 us
  transfers between devices with their start and end apart: 11, of which 11 were waited for; matrix products, arithmetic and copies ran while one was open for 4% of the time, Pallas kernels for 0%

commit v1 on v0

--- a/solution.py
+++ b/solution.py
@@ -6,6 +6,18 @@
 
 SLIDE_BITS = 3
 EPSILON = 1e-06
+
+
+def clear_sides(xin):
+    return jnp.concatenate(
+        lax.all_to_all(
+            jnp.stack([xin for _ in range(lax.axis_size(("tm", "batch")))]),
+            axis_name=("tm", "batch"),
+            split_axis=0,
+            concat_axis=0,
+        ),
+        0,
+    )
 
 
 def spread_2(shard, axis, root):
@@ -77,7 +89,7 @@
     window_size = lax.axis_size("tm")
     position = lax.axis_index("tm")
     up_whole, down_whole = (
-        lax.all_gather(w_up, ("tm", "batch"), axis=0, tiled=True),
+        clear_sides(w_up),
         lax.all_gather(w_down, ("tm", "batch"), axis=0, tiled=True),
     )
 

time: 794 us -> 840 us (1.058)
  waiting for transfers between devices: 678 us -> 708 us
  starting transfers between devices: 6.83 us -> 18.4 us
    all_to_all x0 -> x1, waiting for transfers between devices: none -> 151 us  [clear_sides(): lax.all_to_all(jnp.stack([xin for _ in range(lax.axis_size(('tm', 'batch'...]
    all_gather x1, waiting for transfers between devices: 68 us -> 5.74 us  [per_device(): lax.all_gather(w_down, ('tm', 'batch'), axis=0, tiled=True)]
    all_gather x1 -> x0, waiting for transfers between devices: 58.2 us -> none  [per_device(): lax.all_gather(w_up, ('tm', 'batch'), axis=0, tiled=True)]
    reshape x0 -> x1, local copies, waits for them, and re-layouts: none -> 16.6 us  [clear_sides(): jnp.concatenate(lax.all_to_all(jnp.stack([xin for _ in range(lax.axis_siz...]
    unnamed x26 -> x25, local copies, waits for them, and re-layouts: 35.3 us -> 19.1 us
    all_to_all x0 -> x1, starting transfers between devices: none -> 11.6 us  [clear_sides(): lax.all_to_all(jnp.stack([xin for _ in range(lax.axis_size(('tm', 'batch'...]
where the time goes in v1:
time: 840 us; the launch traced here: 837 us
  waiting for transfers between devices  708 us (84%)
  local copies, waits for them, and re-layouts  41.8 us (5%)
  matrix products  40.5 us (5%)
  starting transfers between devices  18.4 us (2%)
  between operations  14.7 us (2%)
  other arithmetic  14.3 us (2%)
    all_gather x2, waiting for transfers between devices, carried_in(): gathered = lax.all_gather(part, axis)  268 us
    psum x2, waiting for transfers between devices, spread_2(): return lax.psum(jnp.where(mine, shard, jnp.zeros_like(shard)), axis)  180 us
    all_to_all x1, waiting for transfers between devices, clear_sides(): lax.all_to_all(jnp.stack([xin for _ in range(lax.axis_size(('tm', 'batch'...  151 us
    ppermute x5, waiting for transfers between devices, from_behind(): return lax.ppermute(shard, axis, pairs)  102 us
    dot_general x2, matrix products, dense_pair(): return jnp.dot(activated, down_rows, preferred_element_type=jnp.float32)  31.7 us
    unnamed x25, local copies, waits for them, and re-layouts  19.1 us
  transfers between devices with their start and end apart: 11, of which 11 were waited for; matrix products, arithmetic and copies ran while one was open for 4% of the time, Pallas kernels for 0%

profile of v1, /device:TPU:0, one launch (start us, length us, event | category | flops | bytes accessed | tf_op | source)
XLA Modules:
  0.0 837.3 jit_solution(16758103040733630025)
XLA Ops:
  6.5 0.7 all-gather.11.cloned.1.call-update
  7.3 6.0 stack.2
  13.2 11.6 %all-to-all-start = ((bf16[128,36,1152]{2,1,0:T(8,128)(2,1)}), bf16[128,36,1152]{2,1,0:T(8,128)(2,1)}, u32[]{:S(2)}, u32[]{:S(2)}) async-start(bf16[128,36,1152]{2,1,0:T(8,128)(2,1)} %stack.2), calls=%async_computation | async-start | bytes 23592960 | tf_op jit(solution)/shard_map/all_to_all | solution.py:13
  24.9 0.0 all-gather.7.cloned.1.call-start
  26.3 0.1 reduce_sum.73
  26.4 0.1 fusion.84
  26.5 0.7 select_reduce_fusion
  27.2 4.4 fusion.70
  31.7 1.2 fusion.35
  32.9 150.6 %all-to-all-done = bf16[128,36,1152]{2,1,0:T(8,128)(2,1)} async-done(((bf16[128,36,1152]{2,1,0:T(8,128)(2,1)}), bf16[128,36,1152]{2,1,0:T(8,128)(2,1)}, u32[]{:S(2)}, u32[]{:S(2)}) %all-to-all-start) | async-done | bytes 10616864 | tf_op jit(solution)/shard_map/all_to_all | solution.py:13
  183.5 16.6 %reshape.323 = bf16[4608,1152]{1,0:T(8,128)(2,1)} reshape(bf16[128,36,1152]{2,1,0:T(8,128)(2,1)} %all-to-all-done) | data formatting | bytes 21233664 | tf_op jit(solution)/shard_map/reshape | solution.py:12
  200.1 5.7 all-gather.11.cloned.1.call-done
  205.8 16.3 %reshape.329 = bf16[4608,1152]{1,0:T(8,128)(2,1)} reshape(bf16[128,36,1152]{2,1,0:T(8,128)(2,1)} %all-gather.11.cloned.1.call-done) | data formatting | bytes 21233664
  222.1 15.8 %fusion.18 = f32[256,1152]{1,0:T(8,128)} fusion(bf16[4608,1152]{1,0:T(8,128)(2,1)} %reshape.329, f32[1,1,256,1152]{3,2,1,0:T(8,128)S(1)} %copy-done.1, bf16[4608,1152]{1,0:T(8,128)(2,1)} %reshape.323, bf16[2,1,1,256,1152]{4,3,2,1,0:T(8,128)(2,1)S(1)} %copy-done.10, f32[]{:T(128)} %get-tuple-element.86, f32[1152]{0:T(1024)S(1)} %get-tuple-element.82, ...), kind=kOutput, calls=%fused_computation.24 | convolution fusion | flops 5449678848 | bytes 25389064 | tf_op jit(solution)/shard_map/dot_general | solution.py:56
  238.0 0.0 all-reduce.3.cloned.1.call-start
  238.0 0.7 all-reduce.3.cloned.1.call-update
  238.8 120.5 %all-gather.7.cloned.1.call-done = f32[4096,1152]{1,0:T(8,128)} async-done(((f32[256,1152]{1,0:T(8,128)}), f32[4096,1152]{1,0:T(8,128)}) %all-gather.7.cloned.1.call-update) | async-done | bytes 18874384 | tf_op jit(solution)/shard_map/all_gather | solution.py:30
  359.3 0.1 broadcast.245.clone
  359.4 89.9 %all-reduce.3.cloned.1.call-done = f32[1,256,1152]{2,1,0:T(8,128)} async-done(((f32[1,256,1152]{2,1,0:T(8,128)}), f32[1,256,1152]{2,1,0:T(8,128)}) %all-reduce.3.cloned.1.call-update) | async-done | bytes 1179664 | tf_op jit(solution)/shard_map/psum | solution.py:25
  449.3 1.5 add.165
  450.8 1.3 collective-permute-start.2
  452.1 26.8 %collective-permute-done.2 = f32[1,256,1152]{2,1,0:T(8,128)S(1)} collective-permute-done((f32[1,256,1152]{2,1,0:T(8,128)S(1)}, f32[1,256,1152]{2,1,0:T(8,128)S(1)}, u32[]{:S(2)}, u32[]{:S(2)}) %collective-permute-start.2) | collective-permute-done | bytes 1179680 | tf_op jit(solution)/shard_map/ppermute | solution.py:42
  479.0 1.0 copy-done.2
  480.0 2.5 select_select_fusion.2
  482.4 1.3 collective-permute-start.3
  483.7 1.3 collective-permute-start
  485.0 26.1 %collective-permute-done.3 = f32[1,256,1152]{2,1,0:T(8,128)S(1)} collective-permute-done((f32[1,256,1152]{2,1,0:T(8,128)S(1)}, f32[1,256,1152]{2,1,0:T(8,128)S(1)}, u32[]{:S(2)}, u32[]{:S(2)}) %collective-permute-start.3) | collective-permute-done | bytes 1179680 | tf_op jit(solution)/shard_map/ppermute | solution.py:42
  511.1 25.3 %collective-permute-done = f32[1,256,1152]{2,1,0:T(8,128)S(1)} collective-permute-done((f32[1,256,1152]{2,1,0:T(8,128)}, f32[1,256,1152]{2,1,0:T(8,128)S(1)}, u32[]{:S(2)}, u32[]{:S(2)}) %collective-permute-start) | collective-permute-done | bytes 1179680 | tf_op jit(solution)/shard_map/ppermute | solution.py:42
  536.4 1.0 copy-done.5
  537.5 1.9 select_select_fusion.1
  539.3 1.3 collective-permute-start.4
  540.6 1.5 collective-permute-start.1
  542.1 0.1 fusion.82
  542.2 4.4 fusion.68
  546.7 0.6 slice_reduce_fusion.1
  547.3 22.9 %collective-permute-done.4 = f32[1,256,1152]{2,1,0:T(8,128)S(1)} collective-permute-done((f32[1,256,1152]{2,1,0:T(8,128)S(1)}, f32[1,256,1152]{2,1,0:T(8,128)S(1)}, u32[]{:S(2)}, u32[]{:S(2)}) %collective-permute-start.4) | collective-permute-done | bytes 1179680 | tf_op jit(solution)/shard_map/ppermute | solution.py:42
  570.2 0.7 collective-permute-done.1
  570.9 0.3 copy-done.3
  571.2 1.9 fusion.98
  573.1 1.2 multiply_reduce_fusion
  574.4 0.4 copy-done.11
  574.7 15.9 %fusion.22 = f32[1,256,1152]{2,1,0:T(8,128)} fusion(f32[1,256,1152]{2,1,0:T(8,128)S(1)} %get-tuple-element.104, bf16[4608,1152]{1,0:T(8,128)(2,1)} %reshape.329, bf16[4608,1152]{1,0:T(8,128)(2,1)} %reshape.323, bf16[2,1,1,256,1152]{4,3,2,1,0:T(8,128)(2,1)S(1)} %copy-done.11, f32[]{:T(128)} %get-tuple-element.85, f32[1152]{0:T(1024)S(1)} %copy-done.7, ...), kind=kOutput, calls=%fused_computation.28 | convolution fusion | flops 5449678848 | bytes 25389064 | tf_op jit(solution)/shard_map/dot_general | solution.py:56
  590.6 0.0 all-reduce.5.cloned.1.call-start
  590.7 0.5 all-reduce.5.cloned.1.call-update
  591.2 147.3 %all-gather.9.cloned.1.call-done = f32[16,256,1152]{2,1,0:T(8,128)} async-done(((f32[1,256,1152]{2,1,0:T(8,128)}), f32[16,256,1152]{2,1,0:T(8,128)}) %all-gather.9.cloned.1.call-update) | async-done | bytes 18874384 | tf_op jit(solution)/shard_map/all_gather | solution.py:30
  738.5 0.1 broadcast.245
  738.6 89.8 %all-reduce.5.cloned.1.call-done = f32[1,256,1152]{2,1,0:T(8,128)} async-done(((f32[1,256,1152]{2,1,0:T(8,128)}), f32[1,256,1152]{2,1,0:T(8,128)}) %all-reduce.5.cloned.1.call-update) | async-done | bytes 1179664 | tf_op jit(solution)/shard_map/psum | solution.py:25
  828.4 2.4 add_bitcast_fusion
  (31 shorter events, 0.2 us)
Async XLA Ops:
  6.5 199.3 %all-gather.11.cloned.1.call-start = ((), (), s32[]{:S(2)}) async-start(), calls=%async_computation.5 | async-start | bytes 11888640 | tf_op jit(solution)/shard_map/all_gather | solution.py:93
  13.2 13.0 %copy-start.1 = (f32[1,1,256,1152]{3,2,1,0:T(8,128)S(1)}, f32[1,1,256,1152]{3,2,1,0:T(8,128)}, u32[]{:S(2)}) copy-start(f32[1,1,256,1152]{3,2,1,0:T(8,128)} %param.14) | copy-start | bytes 3538948
  13.2 170.3 %all-to-all-start = ((bf16[128,36,1152]{2,1,0:T(8,128)(2,1)}), bf16[128,36,1152]{2,1,0:T(8,128)(2,1)}, u32[]{:S(2)}, u32[]{:S(2)}) async-start(bf16[128,36,1152]{2,1,0:T(8,128)(2,1)} %stack.2), calls=%async_computation | async-start | bytes 23592960 | tf_op jit(solution)/shard_map/all_to_all | solution.py:13
  24.9 1.6 copy-start.8
  24.9 1.6 copy-start.9
  24.9 2.3 copy-start.6
  24.9 334.4 %all-gather.7.cloned.1.call-start = ((), (), s32[]{:S(2)}) async-start(), calls=%async_computation.3 | async-start | bytes 20054016 | tf_op jit(solution)/shard_map/all_gather | solution.py:30
  200.1 22.0 %copy-start.10 = (bf16[2,1,1,256,1152]{4,3,2,1,0:T(8,128)(2,1)S(1)}, bf16[2,1,1,256,1152]{4,3,2,1,0:T(8,128)(2,1)}, u32[]{:S(2)}) copy-start(bf16[2,1,1,256,1152]{4,3,2,1,0:T(8,128)(2,1)} %param.15) | copy-start | bytes 3538948
  238.0 211.4 %all-reduce.3.cloned.1.call-start = ((), (), s32[]{:S(2)}) async-start(), calls=%async_computation.1 | async-start | bytes 2359296 | tf_op jit(solution)/shard_map/psum | solution.py:25
  238.7 499.8 %all-gather.9.cloned.1.call-start = ((), (), s32[]{:S(2)}) async-start(), calls=%async_computation.4 | async-start | bytes 20054016 | tf_op jit(solution)/shard_map/all_gather | solution.py:30
  449.3 30.6 %copy-start = (f32[256,1152]{1,0:T(8,128)S(1)}, f32[256,1152]{1,0:T(8,128)}, u32[]{:S(2)}) copy-start(f32[256,1152]{1,0:T(8,128)} %fusion.18) | copy-start | bytes 3538948
  450.8 28.1 %collective-permute-start.2 = (f32[1,256,1152]{2,1,0:T(8,128)S(1)}, f32[1,256,1152]{2,1,0:T(8,128)S(1)}, u32[]{:S(2)}, u32[]{:S(2)}) collective-permute-start(f32[1,256,1152]{2,1,0:T(8,128)S(1)} %add.165), channel_id=1, source_target_pairs={{8,0},{16,8},{24,16},{32,24},{40,32},{48,40},{56,48},{64,56},{72,6... | collective-permute-start | bytes 3538952 | tf_op jit(solution)/shard_map/ppermute | solution.py:42
  478.9 1.0 copy-start.2
  482.4 28.7 %collective-permute-start.3 = (f32[1,256,1152]{2,1,0:T(8,128)S(1)}, f32[1,256,1152]{2,1,0:T(8,128)S(1)}, u32[]{:S(2)}, u32[]{:S(2)}) collective-permute-start(f32[1,256,1152]{2,1,0:T(8,128)S(1)} %get-tuple-element.107), channel_id=1, source_target_pairs={{16,0},{24,8},{32,16},{40,24},{48,32},{56,40},{64,48},{72,56},{80,... | collective-permute-start | bytes 3538952 | tf_op jit(solution)/shard_map/ppermute | solution.py:42
  483.7 52.7 %collective-permute-start = (f32[1,256,1152]{2,1,0:T(8,128)}, f32[1,256,1152]{2,1,0:T(8,128)S(1)}, u32[]{:S(2)}, u32[]{:S(2)}) collective-permute-start(f32[1,256,1152]{2,1,0:T(8,128)} %get-tuple-element.108), channel_id=1, source_target_pairs={{8,0},{16,8},{24,16},{32,24},{40,32},{48,40},{56,48},{64,56},{72,6... | collective-permute-start | bytes 3538952 | tf_op jit(solution)/shard_map/ppermute | solution.py:42
  511.1 25.3 %copy-start.4 = (f32[1,256,1152]{2,1,0:T(8,128)}, f32[1,256,1152]{2,1,0:T(8,128)S(1)}, u32[]{:S(2)}) copy-start(f32[1,256,1152]{2,1,0:T(8,128)S(1)} %collective-permute-done.3) | copy-start | bytes 3538948
  536.4 1.1 copy-start.5
  539.3 30.8 %collective-permute-start.4 = (f32[1,256,1152]{2,1,0:T(8,128)S(1)}, f32[1,256,1152]{2,1,0:T(8,128)S(1)}, u32[]{:S(2)}, u32[]{:S(2)}) collective-permute-start(f32[1,256,1152]{2,1,0:T(8,128)S(1)} %get-tuple-element.105), channel_id=1, source_target_pairs={{32,0},{40,8},{48,16},{56,24},{64,32},{72,40},{80,48},{88,56},{96,... | collective-permute-start | bytes 3538952 | tf_op jit(solution)/shard_map/ppermute | solution.py:42
  540.6 30.3 %collective-permute-start.1 = (f32[1,256,1152]{2,1,0:T(8,128)S(1)}, f32[1,256,1152]{2,1,0:T(8,128)}, u32[]{:S(2)}, u32[]{:S(2)}) collective-permute-start(f32[1,256,1152]{2,1,0:T(8,128)S(1)} %get-tuple-element.106), channel_id=1, source_target_pairs={{16,0},{24,8},{32,16},{40,24},{48,32},{56,40},{64,48},{72,56},{80,... | collective-permute-start | bytes 3538952 | tf_op jit(solution)/shard_map/ppermute | solution.py:42
  570.2 1.0 copy-start.3
  573.1 1.2 copy-start.7
  573.1 1.6 copy-start.11
  590.6 237.8 %all-reduce.5.cloned.1.call-start = ((), (), s32[]{:S(2)}) async-start(), calls=%async_computation.2 | async-start | bytes 2359296 | tf_op jit(solution)/shard_map/psum | solution.py:25
Sparse Core Ops, SparseCore 0:
  10.3 195.4 all-gather.10
  238.1 121.1 all-gather.6
  362.6 86.6 all-reduce.2
  590.8 147.7 all-gather.8
  741.7 86.6 all-reduce.4
